TPU v7x, 512 devices: a whole 4x4x16 slice. The times are simulated.
512 devices in a mesh: layer: 16 (over z), tile: 32 (over x, y, core).
Axes of the slice: x: 4, y: 4, z: 16, core: 2. Of those that a mesh axis runs over, the one named last changes fastest.
Arguments:
- start: bfloat16 [16, 256, 8192], P(None, 'layer', 'tile'), may hold values from -2.6 to 2.6
- site_weight: float32 [256, 8192], P('layer', 'tile'), may hold values from 0.24 to 4.48, as said below
- onsite: float32 [256, 8192], P('layer', 'tile'), may hold values from -0.5 to 0.5
- hop_right: float32 [256, 8192], P('layer', 'tile'), may hold values from 0.6 to 1.2
- hop_down: float32 [256, 8192], P('layer', 'tile'), may hold values from 0.6 to 1.2
- send_rows: int32 [128, 128, 128], P('layer', 'tile'), may hold values from 0 to 4095
- recv_rows: int32 [128, 128, 128], P('layer', 'tile'), may hold values from 0 to 4095
- block_counts: int32 [128, 32], P('layer', 'tile'), may hold values from 0 to 4, as said below
- inter_blocks: bfloat16 [128, 128, 128, 128], P('layer', 'tile'), may hold values from -0.5 to 0.5
Outputs:
- final_panel: bfloat16 [32, 256, 8192], P(None, 'layer', 'tile')
- moments: float32 [4, 4], replicated
Inputs may be any that keep to these rules, and one draw needn't show every extreme that they name: block_counts[i * 8 + l, t] is exactly 4 for l = i // 2, lies between 1 and 4 for l = i // 2 - 1 and l = i // 2 + 1, and is 0 for every other l: a device couples only to the device i xor 1 of the other layer and that device's two neighbours within its layer. `site_weight`: positive weights.
All inputs are finite; a program needn't handle non-finite values.
Results may differ from a plain program's by a relative error of at most 0.0034.
Values may be sent and summed in bfloat16 or wider, within the bound.
No kernel may reach another device: no remote copies, remote signals or barrier semaphores. Data moves between devices by JAX's collectives and lax.ppermute only.
A program may use at most 64 MiB of HBM per device.

v0:
```python
import jax
import jax.numpy as jnp
from jax import lax
from jax.sharding import PartitionSpec as P

ORDER = 4


def shifted(x, axis, by):
    peers = lax.axis_size(axis)
    pairs = [(i, i + by) for i in range(peers) if 0 <= i + by < peers]
    return lax.ppermute(x, axis, pairs)


def with_halo(block, sides, width):
    for axis, dim in sides:
        count = lax.axis_size(axis)
        forward = [(i, i + 1) for i in range(count - 1)]
        backward = [(target, source) for source, target in forward]
        low = lax.ppermute(
            lax.slice_in_dim(block, block.shape[dim] - width, None, axis=dim), axis, forward
        )
        high = lax.ppermute(lax.slice_in_dim(block, 0, width, axis=dim), axis, backward)
        block = jnp.concatenate([low, block, high], axis=dim)
    return block


def partner(x, axis, stride):
    return lax.ppermute(x, axis, [(i, i ^ 1 << stride) for i in range(lax.axis_size(axis))])


def with_faces(vectors):
    above = shifted(vectors[:, -1:], "layer", 2)
    below = shifted(vectors[:, :1], "layer", -2)
    stacked = jnp.concatenate([above, vectors, below], axis=1)
    return with_halo(stacked, (("tile", 2),), 1)


def apply_velocity(padded, hop_right, hop_left):
    return hop_right * padded[:, 1:-1, 2:] - hop_left * padded[:, 1:-1, :-2]


def in_layer_term(padded, onsite, hop_right, hop_left, bond_down, bond_up):
    centre = padded[:, 1:-1, 1:-1]
    right_cells = padded[:, 1:-1, 2:]
    left_cells = padded[:, 1:-1, :-2]
    lower_cells = padded[:, 2:, 1:-1]
    upper_cells = padded[:, :-2, 1:-1]
    return (
        onsite * centre
        - hop_right * right_cells
        - hop_left * left_cells
        - bond_down * lower_cells
        - bond_up * upper_cells
    )


def inner_sum(first_array, second_array):
    return jnp.sum(first_array * second_array)


def cross_term(vectors, send_rows, recv_rows, block_counts, inter_blocks):
    panel_rows, height, breadth = vectors.shape
    half_size, block_slots, block_rows = send_rows.shape
    position = lax.axis_index("layer")
    lower_index = position // 2
    slot_span = half_size * block_slots * block_rows
    flattened = vectors.reshape(panel_rows, height * breadth)
    selected = jnp.take(flattened, send_rows.reshape(-1), axis=1)
    live_mask = (
        lax.broadcasted_iota(jnp.int32, (half_size, block_slots), 1) < block_counts
    ).astype(jnp.bfloat16)
    outgoing = (
        selected.astype(jnp.bfloat16).reshape(panel_rows, half_size, block_slots, block_rows)
        * live_mask[None, :, :, None]
    )
    widened = jnp.pad(outgoing, ((0, 0), (1, 1), (0, 0), (0, 0)))
    nearby = lax.dynamic_slice_in_dim(widened, lower_index, 3, axis=1)
    across = partner(nearby, "layer", 0)
    from_below = shifted(across[:, 2], "layer", 2)
    from_above = shifted(across[:, 0], "layer", -2)
    gathered = jnp.stack([from_below, across[:, 1], from_above], axis=1)
    holder = jnp.zeros((panel_rows, half_size + 2, block_slots, block_rows), jnp.bfloat16)
    holder = lax.dynamic_update_slice_in_dim(holder, gathered, lower_index, axis=1)
    received = holder[:, 1 : half_size + 1].reshape(panel_rows, slot_span)
    arriving = received.reshape(panel_rows, half_size, block_slots, block_rows)
    products = jnp.einsum(
        "pabk,abkq->pabq", arriving, inter_blocks, preferred_element_type=jnp.float32
    )
    collected = (
        jnp.zeros((panel_rows, height * breadth), jnp.float32)
        .at[:, recv_rows.reshape(-1)]
        .add(products.reshape(panel_rows, slot_span))
    )
    return collected.reshape(panel_rows, height, breadth)


def local(
    start,
    site_weight,
    onsite,
    hop_right,
    hop_down,
    send_rows,
    recv_rows,
    block_counts,
    inter_blocks,
):
    vector_count, height, breadth = start.shape
    half_size = send_rows.shape[0]
    lower_index = lax.axis_index("layer") // 2
    row_index = lax.broadcasted_iota(jnp.int32, (height, breadth), 0)
    col_index = lax.broadcasted_iota(jnp.int32, (height, breadth), 1)
    inside_half = jnp.logical_or(row_index != height - 1, lower_index != half_size - 1)
    bonded = jnp.logical_and((row_index + col_index) % 2 == 0, inside_half)
    bond_down = jnp.where(bonded, hop_down, jnp.zeros_like(hop_down))
    left_column = shifted(hop_right[:, -1:], "tile", 1)
    hop_left = jnp.concatenate([left_column, hop_right[:, :-1]], axis=1)
    upper_row = shifted(bond_down[-1:], "layer", 2)
    bond_up = jnp.concatenate([upper_row, bond_down[:-1]], axis=0)
    right_start = site_weight[None] * start.astype(jnp.float32)
    left_start = apply_velocity(with_faces(right_start), hop_right, hop_left)
    vectors = jnp.concatenate([left_start, right_start], axis=0)
    previous = vectors
    moments = jnp.zeros((ORDER, ORDER), jnp.float32)
    zero_term = jnp.zeros((), jnp.float32)
    left_chain = []
    velocities = []
    for order_step in range(ORDER):
        padded = with_faces(vectors)
        left_chain.append(vectors[:vector_count])
        velocities.append(apply_velocity(padded[vector_count:], hop_right, hop_left))
        row_terms = jnp.stack(
            [
                (
                    inner_sum(left_chain[order_step], velocities[other_index])
                    if other_index <= order_step
                    else zero_term
                )
                for other_index in range(ORDER)
            ]
        )
        column_terms = jnp.stack(
            [
                (
                    inner_sum(left_chain[other_index], velocities[order_step])
                    if other_index < order_step
                    else zero_term
                )
                for other_index in range(ORDER)
            ]
        )
        pair_terms = jnp.stack([row_terms, column_terms])
        pair_terms = lax.psum(pair_terms, ("layer", "tile"))
        moments = moments.at[order_step, :].add(pair_terms[0]).at[:, order_step].add(pair_terms[1])
        in_layer = in_layer_term(padded, onsite, hop_right, hop_left, bond_down, bond_up)
        applied = 0.25 * (
            in_layer + cross_term(vectors, send_rows, recv_rows, block_counts, inter_blocks)
        )
        if order_step == 0:
            advanced = applied
        else:
            advanced = 2.0 * applied - previous
        previous = vectors
        vectors = advanced
    total_cells = vector_count * height * breadth * lax.axis_size("layer") * lax.axis_size("tile")
    return (vectors.astype(jnp.bfloat16), moments * (-0.25 / total_cells))


def solution(mesh):
    return jax.shard_map(
        local,
        mesh=mesh,
        in_specs=(
            P(None, "layer", "tile"),
            P("layer", "tile"),
            P("layer", "tile"),
            P("layer", "tile"),
            P("layer", "tile"),
            P("layer", "tile", None),
            P("layer", "tile", None),
            P("layer", "tile"),
            P("layer", "tile", None, None),
        ),
        out_specs=(P(None, "layer", "tile"), P()),
        check_vma=False,
    )
```

profile of v0, /device:TPU:96, one launch (start us, length us, event | category | flops | bytes accessed | tf_op | source)
XLA Modules:
  0.0 503.3 jit_solution(16459988872291246422)
XLA Ops:
  1.7 6.4 %collective-permute-start = (f32[16,1,256]{2,1,0:T(1,128)S(1)}, f32[16,1,256]{2,1,0:T(1,128)S(1)}, u32[]{:S(2)}, u32[]{:S(2)}) collective-permute-start(f32[16,1,256]{2,1,0:T(1,128)S(1)} %get-tuple-element.151), channel_id=1, source_target_pairs={{0,64},{32,96},{64,128},{96,160},{128,192},{160,224},{192,256},{22... | collective-permute-start | bytes 49160 | tf_op jit(solution)/shard_map/ppermute | solution.py:12
  13.1 5.9 %collective-permute-start.9 = (f32[1,256]{1,0:T(1,128)S(1)}, f32[1,256]{1,0:T(1,128)S(1)}, u32[]{:S(2)}, u32[]{:S(2)}) collective-permute-start(f32[1,256]{1,0:T(1,128)S(1)} %slice.504), channel_id=1, source_target_pairs={{0,64},{32,96},{64,128},{96,160},{128,192},{160,224},{192,256},{22... | collective-permute-start | bytes 3080 | tf_op jit(solution)/shard_map/ppermute | solution.py:12
  28.1 4.6 collective-permute-start.4
  34.7 14.9 %gather_fusion = bf16[4096,32]{1,0:T(8,128)(2,1)} fusion(bf16[32,4096]{0,1:T(8,128)(2,1)S(1)} %bitcast.107, s32[4096]{0:T(1024)S(1)} %fusion.67), kind=kCustom, calls=%fused_computation.clone | custom fusion | bytes 540672 | tf_op jit(solution)/shard_map/jit(_take)/gather | solution.py:69
  51.4 4.6 collective-permute-start.5
  64.9 5.9 %collective-permute-start.11 = (bf16[32,4,128]{2,0,1:T(8,128)(2,1)S(1)}, bf16[32,4,128]{2,0,1:T(8,128)(2,1)S(1)}, u32[]{:S(2)}, u32[]{:S(2)}) collective-permute-start(bf16[32,4,128]{2,0,1:T(8,128)(2,1)S(1)} %get-tuple-element.162), channel_id=1, source_target_pairs={{0,64},{32,96},{64,128},{96,160},{128,192},{160,224},{192,256},{22... | collective-permute-start | bytes 98312 | tf_op jit(solution)/shard_map/ppermute | solution.py:12
  74.8 4.9 collective-permute-start.8
  82.7 24.0 %scatter_custom_fusion = f32[32,4096]{0,1:T(8,128)} fusion(s32[4096]{0:T(1024)} %bitcast.129, f32[4096,32]{1,0:T(8,128)} %copy.55, f32[]{:T(128)} %constant.279.clone.1), kind=kCustom, calls=%fused_computation.18 | custom fusion | flops 131072 | bytes 524800 | tf_op jit(solution)/shard_map/scatter-add | solution.py:93
  113.1 5.9 %collective-permute-start.13 = (f32[32,1,256]{2,1,0:T(1,128)}, f32[32,1,256]{2,1,0:T(1,128)S(1)}, u32[]{:S(2)}, u32[]{:S(2)}) collective-permute-start(f32[32,1,256]{2,1,0:T(1,128)} %get-tuple-element.146), channel_id=1, source_target_pairs={{0,64},{32,96},{64,128},{96,160},{128,192},{160,224},{192,256},{22... | collective-permute-start | bytes 98312 | tf_op jit(solution)/shard_map/ppermute | solution.py:12
  120.9 16.9 %gather_fusion.1 = bf16[4096,32]{1,0:T(8,128)(2,1)} fusion(bf16[32,4096]{0,1:T(8,128)(2,1)} %bitcast.105, s32[4096]{0:T(1024)} %copy-done.20), kind=kCustom, calls=%fused_computation.1.clone | custom fusion | bytes 540672 | tf_op jit(solution)/shard_map/jit(_take)/gather | solution.py:69
  139.7 2.9 collective-permute-start.17
  142.8 3.4 collective-permute-done.17
  146.3 6.0 %collective-permute-start.18 = (bf16[32,4,128]{2,0,1:T(8,128)(2,1)S(1)}, bf16[32,4,128]{2,0,1:T(8,128)(2,1)S(1)}, u32[]{:S(2)}, u32[]{:S(2)}) collective-permute-start(bf16[32,4,128]{2,0,1:T(8,128)(2,1)S(1)} %get-tuple-element.159), channel_id=1, source_target_pairs={{0,64},{32,96},{64,128},{96,160},{128,192},{160,224},{192,256},{22... | collective-permute-start | bytes 98312 | tf_op jit(solution)/shard_map/ppermute | solution.py:12
  156.5 5.0 %collective-permute-start.16 = (f32[32,18,1]{2,1,0:T(8,128)}, f32[32,18,1]{2,1,0:T(8,128)}, u32[]{:S(2)}, u32[]{:S(2)}) collective-permute-start(f32[32,18,1]{2,1,0:T(8,128)} %get-tuple-element.138), channel_id=1, source_target_pairs={{0,1},{1,2},{2,3},{3,4},{4,5},{5,6},{6,7},{7,8},{8,9},{9,10},{10,1... | collective-permute-start | bytes 6920 | tf_op jit(solution)/shard_map/ppermute | solution.py:20
  166.4 24.1 %scatter_custom_fusion.1 = f32[32,4096]{0,1:T(8,128)} fusion(s32[4096]{0:T(1024)} %bitcast.130, f32[4096,32]{1,0:T(8,128)} %copy.61, f32[]{:T(128)} %constant.279.clone.1), kind=kCustom, calls=%fused_computation.16 | custom fusion | flops 131072 | bytes 524800 | tf_op jit(solution)/shard_map/scatter-add | solution.py:93
  190.4 3.0 copy.62
  197.4 5.7 %collective-permute-start.20 = (f32[32,1,256]{2,1,0:T(1,128)}, f32[32,1,256]{2,1,0:T(1,128)}, u32[]{:S(2)}, u32[]{:S(2)}) collective-permute-start(f32[32,1,256]{2,1,0:T(1,128)} %get-tuple-element.144), channel_id=1, source_target_pairs={{0,64},{32,96},{64,128},{96,160},{128,192},{160,224},{192,256},{22... | collective-permute-start | bytes 98312 | tf_op jit(solution)/shard_map/ppermute | solution.py:12
  205.1 16.9 %gather_fusion.2 = bf16[4096,32]{1,0:T(8,128)(2,1)} fusion(bf16[32,4096]{0,1:T(8,128)(2,1)} %bitcast.106, s32[4096]{0:T(1024)} %copy-done.20), kind=kCustom, calls=%fused_computation.2.clone | custom fusion | bytes 540672 | tf_op jit(solution)/shard_map/jit(_take)/gather | solution.py:69
  230.6 4.9 collective-permute-start.23
  235.6 5.7 %collective-permute-start.25 = (bf16[32,4,128]{2,0,1:T(8,128)(2,1)S(1)}, bf16[32,4,128]{2,0,1:T(8,128)(2,1)S(1)}, u32[]{:S(2)}, u32[]{:S(2)}) collective-permute-start(bf16[32,4,128]{2,0,1:T(8,128)(2,1)S(1)} %get-tuple-element.156), channel_id=1, source_target_pairs={{0,64},{32,96},{64,128},{96,160},{128,192},{160,224},{192,256},{22... | collective-permute-start | bytes 98312 | tf_op jit(solution)/shard_map/ppermute | solution.py:12
  245.9 3.9 collective-permute-done.26
  254.6 24.1 %scatter_custom_fusion.2 = f32[32,4096]{0,1:T(8,128)} fusion(s32[4096]{0:T(1024)} %bitcast.131, f32[4096,32]{1,0:T(8,128)} %copy.67, f32[]{:T(128)} %constant.279.clone.1), kind=kCustom, calls=%fused_computation.14 | custom fusion | flops 131072 | bytes 524800 | tf_op jit(solution)/shard_map/scatter-add | solution.py:93
  278.6 3.0 copy.68
  288.1 5.2 %collective-permute-start.28 = (f32[32,1,256]{2,1,0:T(1,128)}, f32[32,1,256]{2,1,0:T(1,128)}, u32[]{:S(2)}, u32[]{:S(2)}) collective-permute-start(f32[32,1,256]{2,1,0:T(1,128)} %get-tuple-element.141), channel_id=1, source_target_pairs={{64,0},{96,32},{128,64},{160,96},{192,128},{224,160},{256,192},{28... | collective-permute-start | bytes 98312 | tf_op jit(solution)/shard_map/ppermute | solution.py:12
  293.3 16.9 %gather_fusion.3 = bf16[4096,32]{1,0:T(8,128)(2,1)} fusion(bf16[32,4096]{0,1:T(8,128)(2,1)} %bitcast.104, s32[4096]{0:T(1024)} %copy-done.20), kind=kCustom, calls=%fused_computation.3.clone | custom fusion | bytes 540672 | tf_op jit(solution)/shard_map/jit(_take)/gather | solution.py:69
  317.9 3.1 collective-permute-start.30
  324.8 3.8 fusion.74
  331.1 3.8 fusion.69
  337.4 116.8 %all-reduce.6 = (f32[2,4]{1,0:T(2,128)S(1)}, f32[2,4]{1,0:T(2,128)S(1)}, f32[2,4]{1,0:T(2,128)S(1)}, f32[2,4]{1,0:T(2,128)S(1)}) all-reduce(f32[2,4]{1,0:T(2,128)S(1)} %stack.153, f32[2,4]{1,0:T(2,128)S(1)} %pad_maximum_fusion.50, f32[2,4]{1,0:T(2,128)S(1)} %pad_maximum_fusion.51, ...), channel_id=1, replica_groups=mesh['layer'=16,'tile'=32] {'layer','tile'}, use_global_device_ids=true, to_apply=%region_5.7 | all-reduce | flops 32 | bytes 256 | tf_op jit(solution)/shard_map/psum | solution.py:154
  457.2 4.6 collective-permute-start.32
  464.5 5.2 %collective-permute-done.33 = bf16[32,4,128]{2,0,1:T(8,128)(2,1)S(1)} collective-permute-done((bf16[32,4,128]{2,0,1:T(8,128)(2,1)S(1)}, bf16[32,4,128]{2,0,1:T(8,128)(2,1)S(1)}, u32[]{:S(2)}, u32[]{:S(2)}) %collective-permute-start.33) | collective-permute-done | bytes 32800 | tf_op jit(solution)/shard_map/ppermute | solution.py:12
  474.5 24.1 %scatter_custom_fusion.3 = f32[32,4096]{0,1:T(8,128)} fusion(s32[4096]{0:T(1024)} %bitcast.132, f32[4096,32]{1,0:T(8,128)} %copy.73, f32[]{:T(128)} %constant.279.clone.1), kind=kCustom, calls=%fused_computation.12 | custom fusion | flops 131072 | bytes 524800 | tf_op jit(solution)/shard_map/scatter-add | solution.py:93
  (238 shorter events, 115.3 us)
Async XLA Ops:
  1.7 24.9 %collective-permute-start = (f32[16,1,256]{2,1,0:T(1,128)S(1)}, f32[16,1,256]{2,1,0:T(1,128)S(1)}, u32[]{:S(2)}, u32[]{:S(2)}) collective-permute-start(f32[16,1,256]{2,1,0:T(1,128)S(1)} %get-tuple-element.151), channel_id=1, source_target_pairs={{0,64},{32,96},{64,128},{96,160},{128,192},{160,224},{192,256},{22... | collective-permute-start | bytes 49160 | tf_op jit(solution)/shard_map/ppermute | solution.py:12
  8.1 18.5 %collective-permute-start.1 = (f32[16,1,256]{2,1,0:T(1,128)S(1)}, f32[16,1,256]{2,1,0:T(1,128)S(1)}, u32[]{:S(2)}, u32[]{:S(2)}) collective-permute-start(f32[16,1,256]{2,1,0:T(1,128)S(1)} %get-tuple-element.152), channel_id=1, source_target_pairs={{64,0},{96,32},{128,64},{160,96},{192,128},{224,160},{256,192},{28... | collective-permute-start | bytes 49160 | tf_op jit(solution)/shard_map/ppermute | solution.py:12
  10.8 15.0 %collective-permute-start.3 = (f32[16,1]{1,0:T(8,128)S(1)}, f32[16,1]{1,0:T(8,128)S(1)}, u32[]{:S(2)}, u32[]{:S(2)}) collective-permute-start(f32[16,1]{1,0:T(8,128)S(1)} %slice.406), channel_id=1, source_target_pairs={{0,1},{1,2},{2,3},{3,4},{4,5},{5,6},{6,7},{7,8},{8,9},{9,10},{10,1... | collective-permute-start | bytes 200 | tf_op jit(solution)/shard_map/ppermute | solution.py:12
  13.1 19.6 %collective-permute-start.9 = (f32[1,256]{1,0:T(1,128)S(1)}, f32[1,256]{1,0:T(1,128)S(1)}, u32[]{:S(2)}, u32[]{:S(2)}) collective-permute-start(f32[1,256]{1,0:T(1,128)S(1)} %slice.504), channel_id=1, source_target_pairs={{0,64},{32,96},{64,128},{96,160},{128,192},{160,224},{192,256},{22... | collective-permute-start | bytes 3080 | tf_op jit(solution)/shard_map/ppermute | solution.py:12
  26.8 6.5 %collective-permute-start.2 = (f32[16,18,1]{2,1,0:T(8,128)S(1)}, f32[16,18,1]{2,1,0:T(8,128)S(1)}, u32[]{:S(2)}, u32[]{:S(2)}) collective-permute-start(f32[16,18,1]{2,1,0:T(8,128)S(1)} %get-tuple-element.149), channel_id=1, source_target_pairs={{1,0},{2,1},{3,2},{4,3},{5,4},{6,5},{7,6},{8,7},{9,8},{10,9},{11,1... | collective-permute-start | bytes 3464 | tf_op jit(solution)/shard_map/ppermute | solution.py:23
  28.1 5.6 %collective-permute-start.4 = (f32[16,18,1]{2,1,0:T(8,128)S(1)}, f32[16,18,1]{2,1,0:T(8,128)S(1)}, u32[]{:S(2)}, u32[]{:S(2)}) collective-permute-start(f32[16,18,1]{2,1,0:T(8,128)S(1)} %get-tuple-element.150), channel_id=1, source_target_pairs={{0,1},{1,2},{2,3},{3,4},{4,5},{5,6},{6,7},{7,8},{8,9},{9,10},{10,1... | collective-permute-start | bytes 3464 | tf_op jit(solution)/shard_map/ppermute | solution.py:20
  51.4 9.7 %collective-permute-start.5 = (f32[32,1,256]{2,1,0:T(1,128)S(1)}, f32[32,1,256]{2,1,0:T(1,128)S(1)}, u32[]{:S(2)}, u32[]{:S(2)}) collective-permute-start(f32[32,1,256]{2,1,0:T(1,128)S(1)} %get-tuple-element.148), channel_id=1, source_target_pairs={{0,64},{32,96},{64,128},{96,160},{128,192},{160,224},{192,256},{22... | collective-permute-start | bytes 98312 | tf_op jit(solution)/shard_map/ppermute | solution.py:12
  56.1 7.9 %collective-permute-start.6 = (f32[32,1,256]{2,1,0:T(1,128)S(1)}, f32[32,1,256]{2,1,0:T(1,128)S(1)}, u32[]{:S(2)}, u32[]{:S(2)}) collective-permute-start(f32[32,1,256]{2,1,0:T(1,128)S(1)} %get-tuple-element.147), channel_id=1, source_target_pairs={{64,0},{96,32},{128,64},{160,96},{192,128},{224,160},{256,192},{28... | collective-permute-start | bytes 98312 | tf_op jit(solution)/shard_map/ppermute | solution.py:12
  58.3 6.5 %collective-permute-start.10 = (bf16[32,3,4,128]{3,0,2,1:T(8,128)(2,1)S(1)}, bf16[32,3,4,128]{3,0,2,1:T(8,128)(2,1)S(1)}, u32[]{:S(2)}, u32[]{:S(2)}) collective-permute-start(bf16[32,3,4,128]{3,0,2,1:T(8,128)(2,1)S(1)} %pad_dynamic-slice_fusion.3), channel_id=1, source_target_pairs={{0,32},{32,0},{64,96},{96,64},{128,160},{160,128},{192,224},{224,1... | collective-permute-start | bytes 294920 | tf_op jit(solution)/shard_map/ppermute | solution.py:29
  64.9 14.8 %collective-permute-start.11 = (bf16[32,4,128]{2,0,1:T(8,128)(2,1)S(1)}, bf16[32,4,128]{2,0,1:T(8,128)(2,1)S(1)}, u32[]{:S(2)}, u32[]{:S(2)}) collective-permute-start(bf16[32,4,128]{2,0,1:T(8,128)(2,1)S(1)} %get-tuple-element.162), channel_id=1, source_target_pairs={{0,64},{32,96},{64,128},{96,160},{128,192},{160,224},{192,256},{22... | collective-permute-start | bytes 98312 | tf_op jit(solution)/shard_map/ppermute | solution.py:12
  70.7 8.9 %collective-permute-start.12 = (bf16[32,4,128]{2,0,1:T(8,128)(2,1)S(1)}, bf16[32,4,128]{2,0,1:T(8,128)(2,1)S(1)}, u32[]{:S(2)}, u32[]{:S(2)}) collective-permute-start(bf16[32,4,128]{2,0,1:T(8,128)(2,1)S(1)} %get-tuple-element.163), channel_id=1, source_target_pairs={{64,0},{96,32},{128,64},{160,96},{192,128},{224,160},{256,192},{28... | collective-permute-start | bytes 98312 | tf_op jit(solution)/shard_map/ppermute | solution.py:12
  73.5 35.5 %collective-permute-start.7 = (f32[32,18,1]{2,1,0:T(8,128)}, f32[32,18,1]{2,1,0:T(8,128)S(1)}, u32[]{:S(2)}, u32[]{:S(2)}) collective-permute-start(f32[32,18,1]{2,1,0:T(8,128)} %get-tuple-element.139), channel_id=1, source_target_pairs={{1,0},{2,1},{3,2},{4,3},{5,4},{6,5},{7,6},{8,7},{9,8},{10,9},{11,1... | collective-permute-start | bytes 6920 | tf_op jit(solution)/shard_map/ppermute | solution.py:23
  74.8 34.2 %collective-permute-start.8 = (f32[32,18,1]{2,1,0:T(8,128)S(1)}, f32[32,18,1]{2,1,0:T(8,128)}, u32[]{:S(2)}, u32[]{:S(2)}) collective-permute-start(f32[32,18,1]{2,1,0:T(8,128)S(1)} %get-tuple-element.140), channel_id=1, source_target_pairs={{0,1},{1,2},{2,3},{3,4},{4,5},{5,6},{6,7},{7,8},{8,9},{9,10},{10,1... | collective-permute-start | bytes 6920 | tf_op jit(solution)/shard_map/ppermute | solution.py:20
  113.1 29.6 %collective-permute-start.13 = (f32[32,1,256]{2,1,0:T(1,128)}, f32[32,1,256]{2,1,0:T(1,128)S(1)}, u32[]{:S(2)}, u32[]{:S(2)}) collective-permute-start(f32[32,1,256]{2,1,0:T(1,128)} %get-tuple-element.146), channel_id=1, source_target_pairs={{0,64},{32,96},{64,128},{96,160},{128,192},{160,224},{192,256},{22... | collective-permute-start | bytes 98312 | tf_op jit(solution)/shard_map/ppermute | solution.py:12
  118.9 23.8 %collective-permute-start.14 = (f32[32,1,256]{2,1,0:T(1,128)}, f32[32,1,256]{2,1,0:T(1,128)S(1)}, u32[]{:S(2)}, u32[]{:S(2)}) collective-permute-start(f32[32,1,256]{2,1,0:T(1,128)} %get-tuple-element.145), channel_id=1, source_target_pairs={{64,0},{96,32},{128,64},{160,96},{192,128},{224,160},{256,192},{28... | collective-permute-start | bytes 98312 | tf_op jit(solution)/shard_map/ppermute | solution.py:12
  139.7 6.5 %collective-permute-start.17 = (bf16[32,3,4,128]{3,0,2,1:T(8,128)(2,1)S(1)}, bf16[32,3,4,128]{3,0,2,1:T(8,128)(2,1)S(1)}, u32[]{:S(2)}, u32[]{:S(2)}) collective-permute-start(bf16[32,3,4,128]{3,0,2,1:T(8,128)(2,1)S(1)} %pad_dynamic-slice_fusion.2), channel_id=1, source_target_pairs={{0,32},{32,0},{64,96},{96,64},{128,160},{160,128},{192,224},{224,1... | collective-permute-start | bytes 294920 | tf_op jit(solution)/shard_map/ppermute | solution.py:29
  146.3 15.3 %collective-permute-start.18 = (bf16[32,4,128]{2,0,1:T(8,128)(2,1)S(1)}, bf16[32,4,128]{2,0,1:T(8,128)(2,1)S(1)}, u32[]{:S(2)}, u32[]{:S(2)}) collective-permute-start(bf16[32,4,128]{2,0,1:T(8,128)(2,1)S(1)} %get-tuple-element.159), channel_id=1, source_target_pairs={{0,64},{32,96},{64,128},{96,160},{128,192},{160,224},{192,256},{22... | collective-permute-start | bytes 98312 | tf_op jit(solution)/shard_map/ppermute | solution.py:12
  152.3 9.3 %collective-permute-start.19 = (bf16[32,4,128]{2,0,1:T(8,128)(2,1)S(1)}, bf16[32,4,128]{2,0,1:T(8,128)(2,1)S(1)}, u32[]{:S(2)}, u32[]{:S(2)}) collective-permute-start(bf16[32,4,128]{2,0,1:T(8,128)(2,1)S(1)} %get-tuple-element.160), channel_id=1, source_target_pairs={{64,0},{96,32},{128,64},{160,96},{192,128},{224,160},{256,192},{28... | collective-permute-start | bytes 98312 | tf_op jit(solution)/shard_map/ppermute | solution.py:12
  155.2 38.2 %collective-permute-start.15 = (f32[32,18,1]{2,1,0:T(8,128)}, f32[32,18,1]{2,1,0:T(8,128)S(1)}, u32[]{:S(2)}, u32[]{:S(2)}) collective-permute-start(f32[32,18,1]{2,1,0:T(8,128)} %get-tuple-element.137), channel_id=1, source_target_pairs={{1,0},{2,1},{3,2},{4,3},{5,4},{6,5},{7,6},{8,7},{9,8},{10,9},{11,1... | collective-permute-start | bytes 6920 | tf_op jit(solution)/shard_map/ppermute | solution.py:23
  156.5 37.0 %collective-permute-start.16 = (f32[32,18,1]{2,1,0:T(8,128)}, f32[32,18,1]{2,1,0:T(8,128)}, u32[]{:S(2)}, u32[]{:S(2)}) collective-permute-start(f32[32,18,1]{2,1,0:T(8,128)} %get-tuple-element.138), channel_id=1, source_target_pairs={{0,1},{1,2},{2,3},{3,4},{4,5},{5,6},{6,7},{7,8},{8,9},{9,10},{10,1... | collective-permute-start | bytes 6920 | tf_op jit(solution)/shard_map/ppermute | solution.py:20
  197.4 30.8 %collective-permute-start.20 = (f32[32,1,256]{2,1,0:T(1,128)}, f32[32,1,256]{2,1,0:T(1,128)}, u32[]{:S(2)}, u32[]{:S(2)}) collective-permute-start(f32[32,1,256]{2,1,0:T(1,128)} %get-tuple-element.144), channel_id=1, source_target_pairs={{0,64},{32,96},{64,128},{96,160},{128,192},{160,224},{192,256},{22... | collective-permute-start | bytes 98312 | tf_op jit(solution)/shard_map/ppermute | solution.py:12
  203.1 25.1 %collective-permute-start.21 = (f32[32,1,256]{2,1,0:T(1,128)}, f32[32,1,256]{2,1,0:T(1,128)}, u32[]{:S(2)}, u32[]{:S(2)}) collective-permute-start(f32[32,1,256]{2,1,0:T(1,128)} %get-tuple-element.143), channel_id=1, source_target_pairs={{64,0},{96,32},{128,64},{160,96},{192,128},{224,160},{256,192},{28... | collective-permute-start | bytes 98312 | tf_op jit(solution)/shard_map/ppermute | solution.py:12
  225.3 10.2 %collective-permute-start.24 = (bf16[32,3,4,128]{3,0,2,1:T(8,128)(2,1)S(1)}, bf16[32,3,4,128]{3,0,2,1:T(8,128)(2,1)S(1)}, u32[]{:S(2)}, u32[]{:S(2)}) collective-permute-start(bf16[32,3,4,128]{3,0,2,1:T(8,128)(2,1)S(1)} %pad_dynamic-slice_fusion.1), channel_id=1, source_target_pairs={{0,32},{32,0},{64,96},{96,64},{128,160},{160,128},{192,224},{224,1... | collective-permute-start | bytes 294920 | tf_op jit(solution)/shard_map/ppermute | solution.py:29
  229.3 13.9 %collective-permute-start.22 = (f32[32,18,1]{2,1,0:T(8,128)S(1)}, f32[32,18,1]{2,1,0:T(8,128)S(1)}, u32[]{:S(2)}, u32[]{:S(2)}) collective-permute-start(f32[32,18,1]{2,1,0:T(8,128)S(1)} %get-tuple-element.135), channel_id=1, source_target_pairs={{1,0},{2,1},{3,2},{4,3},{5,4},{6,5},{7,6},{8,7},{9,8},{10,9},{11,1... | collective-permute-start | bytes 6920 | tf_op jit(solution)/shard_map/ppermute | solution.py:23
  230.6 12.7 %collective-permute-start.23 = (f32[32,18,1]{2,1,0:T(8,128)S(1)}, f32[32,18,1]{2,1,0:T(8,128)S(1)}, u32[]{:S(2)}, u32[]{:S(2)}) collective-permute-start(f32[32,18,1]{2,1,0:T(8,128)S(1)} %get-tuple-element.136), channel_id=1, source_target_pairs={{0,1},{1,2},{2,3},{3,4},{4,5},{5,6},{6,7},{7,8},{8,9},{9,10},{10,1... | collective-permute-start | bytes 6920 | tf_op jit(solution)/shard_map/ppermute | solution.py:20
  235.6 10.3 %collective-permute-start.25 = (bf16[32,4,128]{2,0,1:T(8,128)(2,1)S(1)}, bf16[32,4,128]{2,0,1:T(8,128)(2,1)S(1)}, u32[]{:S(2)}, u32[]{:S(2)}) collective-permute-start(bf16[32,4,128]{2,0,1:T(8,128)(2,1)S(1)} %get-tuple-element.156), channel_id=1, source_target_pairs={{0,64},{32,96},{64,128},{96,160},{128,192},{160,224},{192,256},{22... | collective-permute-start | bytes 98312 | tf_op jit(solution)/shard_map/ppermute | solution.py:12
  241.3 8.4 %collective-permute-start.26 = (bf16[32,4,128]{2,0,1:T(8,128)(2,1)S(1)}, bf16[32,4,128]{2,0,1:T(8,128)(2,1)S(1)}, u32[]{:S(2)}, u32[]{:S(2)}) collective-permute-start(bf16[32,4,128]{2,0,1:T(8,128)(2,1)S(1)} %get-tuple-element.157), channel_id=1, source_target_pairs={{64,0},{96,32},{128,64},{160,96},{192,128},{224,160},{256,192},{28... | collective-permute-start | bytes 98312 | tf_op jit(solution)/shard_map/ppermute | solution.py:12
  285.8 29.7 %collective-permute-start.27 = (f32[32,1,256]{2,1,0:T(1,128)}, f32[32,1,256]{2,1,0:T(1,128)}, u32[]{:S(2)}, u32[]{:S(2)}) collective-permute-start(f32[32,1,256]{2,1,0:T(1,128)} %get-tuple-element.142), channel_id=1, source_target_pairs={{0,64},{32,96},{64,128},{96,160},{128,192},{160,224},{192,256},{22... | collective-permute-start | bytes 98312 | tf_op jit(solution)/shard_map/ppermute | solution.py:12
  288.1 27.4 %collective-permute-start.28 = (f32[32,1,256]{2,1,0:T(1,128)}, f32[32,1,256]{2,1,0:T(1,128)}, u32[]{:S(2)}, u32[]{:S(2)}) collective-permute-start(f32[32,1,256]{2,1,0:T(1,128)} %get-tuple-element.141), channel_id=1, source_target_pairs={{64,0},{96,32},{128,64},{160,96},{192,128},{224,160},{256,192},{28... | collective-permute-start | bytes 98312 | tf_op jit(solution)/shard_map/ppermute | solution.py:12
  334.9 122.2 %collective-permute-start.31 = (bf16[32,3,4,128]{3,0,2,1:T(8,128)(2,1)}, bf16[32,3,4,128]{3,0,2,1:T(8,128)(2,1)S(1)}, u32[]{:S(2)}, u32[]{:S(2)}) collective-permute-start(bf16[32,3,4,128]{3,0,2,1:T(8,128)(2,1)} %pad_dynamic-slice_fusion), channel_id=1, source_target_pairs={{0,32},{32,0},{64,96},{96,64},{128,160},{160,128},{192,224},{224,1... | collective-permute-start | bytes 294920 | tf_op jit(solution)/shard_map/ppermute | solution.py:29
  457.2 7.3 %collective-permute-start.32 = (bf16[32,4,128]{2,0,1:T(8,128)(2,1)S(1)}, bf16[32,4,128]{2,0,1:T(8,128)(2,1)S(1)}, u32[]{:S(2)}, u32[]{:S(2)}) collective-permute-start(bf16[32,4,128]{2,0,1:T(8,128)(2,1)S(1)} %get-tuple-element.153), channel_id=1, source_target_pairs={{0,64},{32,96},{64,128},{96,160},{128,192},{160,224},{192,256},{22... | collective-permute-start | bytes 98312 | tf_op jit(solution)/shard_map/ppermute | solution.py:12
  461.8 7.9 %collective-permute-start.33 = (bf16[32,4,128]{2,0,1:T(8,128)(2,1)S(1)}, bf16[32,4,128]{2,0,1:T(8,128)(2,1)S(1)}, u32[]{:S(2)}, u32[]{:S(2)}) collective-permute-start(bf16[32,4,128]{2,0,1:T(8,128)(2,1)S(1)} %get-tuple-element.154), channel_id=1, source_target_pairs={{64,0},{96,32},{128,64},{160,96},{192,128},{224,160},{256,192},{28... | collective-permute-start | bytes 98312 | tf_op jit(solution)/shard_map/ppermute | solution.py:12
  (37 other events, 753.2 us)
where the time goes:
time: 507 us; the launch traced here: 503 us
  other arithmetic  139 us (27%)
  blocking collectives  117 us (23%)
  starting transfers between devices  115 us (23%)
  local copies, waits for them, and re-layouts  112 us (22%)
  waiting for transfers between devices  17.2 us (3%)
    psum x1, blocking collectives, local(): pair_terms = lax.psum(pair_terms, ('layer', 'tile'))  117 us
    scatter-add x4, other arithmetic, cross_term(): collected = jnp.zeros((panel_rows, height * breadth), jnp.float32).at[:,...  96.2 us
    ppermute x20, starting transfers between devices, shifted(): return lax.ppermute(x, axis, pairs)  75.4 us
    gather x8, local copies, waits for them, and re-layouts, cross_term(): selected = jnp.take(flattened, send_rows.reshape(-1), axis=1)  71.8 us
    ppermute x5, starting transfers between devices, with_halo(): lax.ppermute(lax.slice_in_dim(block, block.shape[dim] - width, None, axis...  22.5 us
    ppermute x20, waiting for transfers between devices, shifted(): return lax.ppermute(x, axis, pairs)  12 us
    reshape x8, local copies, waits for them, and re-layouts, cross_term(): products.reshape(panel_rows, slot_span)  11.7 us
    ppermute x4, starting transfers between devices, partner(): lax.ppermute(x, axis, [(i, i ^ 1 << stride) for i in range(lax.axis_size(...  11 us
  transfers between devices with their start and end apart: 34, of which 7 were waited for; matrix products, arithmetic and copies ran while one was open for 28% of the time, Pallas kernels for 0%

commit v1 on v0

v1 whole, which is shorter than its diff:
```python
import functools

import jax
import jax.numpy as jnp
from jax import lax
from jax.experimental import pallas as pl
from jax.experimental.pallas import tpu as pltpu
from jax.sharding import PartitionSpec as P

ORDER = 4
F32 = jnp.float32
BF16 = jnp.bfloat16
NT = (((1,), (1,)), ((), ()))
TN = (((0,), (0,)), ((), ()))


def dot(a, b, dims=(((1,), (0,)), ((), ()))):
    return lax.dot_general(a, b, dims, preferred_element_type=F32)


def call(body, outs, scratch=(), scalars=1):
    def run(*args):
        specs = [
            pl.BlockSpec(memory_space=pltpu.SMEM if i < scalars else pltpu.VMEM)
            for i in range(len(args))
        ]
        return pl.pallas_call(
            body,
            out_shape=outs,
            in_specs=specs,
            out_specs=jax.tree.map(lambda _: pl.BlockSpec(memory_space=pltpu.VMEM), outs),
            scratch_shapes=list(scratch),
            compiler_params=pltpu.CompilerParams(vmem_limit_bytes=24 * 1024 * 1024),
        )(*args)

    return run


def unit_rows(places, breadth, rows=16):
    row = lax.broadcasted_iota(jnp.int32, (rows, breadth), 0)
    col = lax.broadcasted_iota(jnp.int32, (rows, breadth), 1)
    hit = jnp.zeros((rows, breadth), F32)
    for r, place in places.items():
        hit = jnp.where(jnp.logical_and(row == r, col == place), 1.0, hit)
    return hit.astype(BF16)


def rim_columns(info_ref, breadth):
    even = info_ref[0] == 0
    core = jnp.where(even, breadth - 1, 0)
    other = jnp.where(even, 0, breadth - 1)
    return core, other


def bonds(hop_down_ref, x):
    row = hop_down_ref[x : x + 1, :]
    col = lax.broadcasted_iota(jnp.int32, row.shape, 1)
    return jnp.where((col + x) % 2 == 0, row, 0.0)


def one_hot_columns(row, height):
    wide = lax.broadcasted_iota(jnp.int32, (height, row.shape[1]), 0)
    return jnp.where(wide == row, 1.0, 0.0).astype(BF16)


def sides(cells, rim):
    breadth = cells.shape[1]
    col = lax.broadcasted_iota(jnp.int32, cells.shape, 1)
    right = jnp.where(col == breadth - 1, rim, pltpu.roll(cells, breadth - 1, 1))
    left = jnp.where(col == 0, rim, pltpu.roll(cells, 1, 1))
    return right, left


def pre_body(info_ref, start_ref, weight_ref, hop_ref, core_ref, other_ref):
    height, count, breadth = start_ref.shape
    even = info_ref[0] == 0
    value, ahead, behind, hop_hi, hop_lo = [], [], [], [], []
    for x in range(height):
        right = weight_ref[x : x + 1, :] * start_ref[x].astype(F32)
        hop = jnp.broadcast_to(hop_ref[x : x + 1, :], right.shape)
        value.append(right.astype(BF16))
        ahead.append((hop * pltpu.roll(right, breadth - 1, 1)).astype(BF16))
        behind.append((hop * right).astype(BF16))
        hi = hop.astype(BF16)
        hop_hi.append(hi)
        hop_lo.append((hop - hi.astype(F32)).astype(BF16))
    value, ahead, behind, hop_hi, hop_lo = (
        jnp.concatenate(part, axis=0) for part in (value, ahead, behind, hop_hi, hop_lo)
    )
    last = breadth - 1
    to_left = dot(unit_rows({0: 0}, breadth), value, NT) + dot(
        unit_rows({1: 0}, breadth), ahead, NT
    )
    to_right = (
        dot(unit_rows({0: last}, breadth), value, NT)
        + dot(unit_rows({1: last - 1}, breadth), behind, NT)
        + dot(unit_rows({2: last}, breadth), hop_hi, NT)
        + dot(unit_rows({3: last}, breadth), hop_lo, NT)
    )
    core_ref[...] = jnp.where(even, to_right, to_left).astype(BF16)
    other_ref[...] = jnp.where(even, to_left, to_right).astype(BF16)


def gather_out(cells_ref, index_ref, out_ref):
    height, count, breadth = cells_ref.shape
    flat = cells_ref[...].reshape(height * count, breadth)
    for begin in range(0, index_ref.shape[1], 256):
        span = slice(begin, begin + 256)
        picked = dot(flat, one_hot_columns(index_ref[1:2, span], breadth))
        which = index_ref[0:1, span]
        total = jnp.zeros((count, 256), F32)
        for x in range(height):
            total = total + jnp.where(which == x, picked[x * count : (x + 1) * count], 0.0)
        out_ref[:, span] = total.astype(BF16)


def y_terms(x, cells, rim, above, below, fields):
    onsite_ref, hop_ref, left_ref, hop_down_ref = fields
    right, left = sides(cells, rim)
    flow_right = hop_ref[x : x + 1, :] * right
    flow_left = left_ref[x : x + 1, :] * left
    term = onsite_ref[x : x + 1, :] * cells - flow_right - flow_left
    if below is not None:
        term = term - bonds(hop_down_ref, x) * below
    if above is not None:
        term = term - bonds(hop_down_ref, x - 1) * above
    half = cells.shape[0] // 2
    return term, flow_right[half:] - flow_left[half:]


def init_body(
    info_ref,
    start_ref,
    weight_ref,
    onsite_ref,
    hop_ref,
    hop_down_ref,
    core_ref,
    other_ref,
    index_ref,
    panel_ref,
    left_ref,
    term_ref,
    flow_ref,
    out_ref,
    up_ref,
    down_ref,
    cells_ref,
):
    height, count, breadth = start_ref.shape
    core, other = rim_columns(info_ref, breadth)
    inner = info_ref[1].astype(F32)
    core_rows, other_rows = core_ref[...], other_ref[...]

    def spread(row):
        wide = dot(core_rows, unit_rows({row: core}, breadth), TN) + dot(
            other_rows, unit_rows({row: other}, breadth), TN
        )
        return wide.reshape(height, count, breadth)

    rim_right = spread(0)
    rim_part = spread(1)
    first = unit_rows({2: 0, 3: 0}, breadth)
    hop_first = (dot(core_rows, first, TN) + dot(other_rows, first, TN)).reshape(
        height, count, breadth
    )
    col = lax.broadcasted_iota(jnp.int32, (count, breadth), 1)
    rims = []
    for x in range(height):
        right_cells = weight_ref[x : x + 1, :] * start_ref[x].astype(F32)
        hop = hop_ref[x : x + 1, :]
        entry = hop_first[x][0:1, :]
        hop_left = jnp.where(col[0:1] == 0, entry, pltpu.roll(jnp.broadcast_to(hop, (8, breadth)), 1, 1)[0:1])
        left_ref[x : x + 1, :] = hop_left
        right, left = sides(right_cells, rim_right[x])
        left_cells = hop * right - hop_left * left
        rim_left = jnp.where(
            col == breadth - 1,
            inner * (rim_part[x] - hop * right_cells),
            jnp.where(col == 0, hop_left * right_cells - rim_part[x], 0.0),
        )
        rims.append(jnp.concatenate([rim_left, rim_right[x]], axis=0))
        cells = jnp.concatenate([left_cells, right_cells], axis=0)
        panel_ref[x] = cells
        cells_ref[x] = cells.astype(BF16)
    gather_out(cells_ref, index_ref, out_ref)
    up_ref[:, :breadth] = cells_ref[height - 1]
    down_ref[...] = cells_ref[0]
    last = bonds(hop_down_ref, height - 1)
    hi = last.astype(BF16).astype(F32)
    row = lax.broadcasted_iota(jnp.int32, (2 * count, breadth), 0)
    extra = jnp.where(row == 0, hi, jnp.where(row == 1, last - hi, 0.0))
    up_ref[:, breadth:] = extra.astype(BF16)
    fields = (onsite_ref, hop_ref, left_ref, hop_down_ref)
    for x in range(height):
        above = panel_ref[x - 1] if x > 0 else None
        below = panel_ref[x + 1] if x < height - 1 else None
        term, flow = y_terms(x, panel_ref[x], rims[x], above, below, fields)
        term_ref[x] = term
        flow_ref[x] = flow


def near_body(
    info_ref, panel_ref, onsite_ref, hop_ref, left_ref, hop_down_ref, core_ref, other_ref,
    term_ref, flow_ref,
):
    height, count, breadth = panel_ref.shape
    core, other = rim_columns(info_ref, breadth)
    rims = dot(core_ref[...], unit_rows({0: core}, breadth), TN) + dot(
        other_ref[...], unit_rows({0: other}, breadth), TN
    )
    fields = (onsite_ref, hop_ref, left_ref, hop_down_ref)
    for x in range(height):
        above = panel_ref[x - 1] if x > 0 else None
        below = panel_ref[x + 1] if x < height - 1 else None
        rim = rims[x * count : (x + 1) * count]
        term, flow = y_terms(x, panel_ref[x], rim, above, below, fields)
        term_ref[x] = term
        flow_ref[x] = flow


def moment_body(*refs):
    panels, flows, out_ref = refs[:ORDER], refs[ORDER : 2 * ORDER], refs[2 * ORDER]
    height, count, breadth = flows[0].shape
    totals = {}
    for x in range(height):
        lefts = [p[x, 0:count, :] for p in panels]
        rights = [f[x] for f in flows]
        for m in range(ORDER):
            for n in range(ORDER):
                term = lefts[m] * rights[n]
                part = term[:, 0:128]
                for begin in range(128, breadth, 128):
                    part = part + term[:, begin : begin + 128]
                folded = part[0:8]
                for begin in range(8, count, 8):
                    folded = folded + part[begin : begin + 8]
                totals[m, n] = folded + totals[m, n] if x else folded
    for m in range(ORDER):
        for n in range(ORDER):
            place = m * ORDER + n
            out_ref[place : place + 1, :] = jnp.sum(totals[m, n], axis=0, keepdims=True)


def far_body(
    step,
    info_ref,
    term_ref,
    prev_ref,
    partner_ref,
    above_ref,
    below_ref,
    bond_ref,
    hop_down_ref,
    blocks_ref,
    index_ref,
    *rest,
):
    last_step = step == ORDER - 1
    if last_step:
        final_ref, lhs_ref, = rest
    else:
        panel_ref, out_ref, core_ref, other_ref, up_ref, down_ref, lhs_ref, cells_ref = rest
    height, count, breadth = term_ref.shape
    total_span = index_ref.shape[1]
    part_span = total_span // 3
    blk = blocks_ref.shape[1]
    for d in range(3):
        for b in range(part_span // blk):
            begin = b * blk
            if d == 0:
                arriving = above_ref[:, begin : begin + blk]
            elif d == 1:
                arriving = partner_ref[:, part_span + begin : part_span + begin + blk]
            else:
                arriving = below_ref[:, begin : begin + blk]
            product = dot(arriving, blocks_ref[d * (part_span // blk) + b])
            place = d * part_span + begin
            which = index_ref[2:3, place : place + blk]
            for x in range(height):
                lhs_ref[x, :, place : place + blk] = jnp.where(which == x, product, 0.0).astype(BF16)
    targets = one_hot_columns(index_ref[3:4, :], breadth)
    crossing = dot(lhs_ref[...].reshape(height * count, total_span), targets, NT)
    bond_up = bond_ref[0:1, part_span + breadth :].astype(F32) + bond_ref[
        1:2, part_span + breadth :
    ].astype(F32)
    for x in range(height):
        term = term_ref[x] + crossing[x * count : (x + 1) * count]
        if x == 0:
            term = term - bond_up * above_ref[:, part_span : part_span + breadth].astype(F32)
        if x == height - 1:
            term = term - bonds(hop_down_ref, x) * below_ref[
                :, part_span : part_span + breadth
            ].astype(F32)
        if step == 0:
            cells = 0.25 * term
        else:
            cells = 0.5 * term - prev_ref[x]
        if last_step:
            final_ref[x] = cells.astype(BF16)
        else:
            panel_ref[x] = cells
            cells_ref[x] = cells.astype(BF16)
    if last_step:
        return
    gather_out(cells_ref, index_ref, out_ref)
    core, other = rim_columns(info_ref, breadth)
    flat = cells_ref[...].reshape(height * count, breadth)
    core_ref[...] = dot(unit_rows({0: core}, breadth), flat, NT).astype(BF16)
    other_ref[...] = dot(unit_rows({0: other}, breadth), flat, NT).astype(BF16)
    up_ref[...] = cells_ref[height - 1]
    down_ref[...] = cells_ref[0]


def shifted(x, axis, by):
    peers = lax.axis_size(axis)
    pairs = [(i, i + by) for i in range(peers) if 0 <= i + by < peers]
    return lax.ppermute(x, axis, pairs)


def tile_swaps(core, other):
    peers = lax.axis_size("tile")
    got_core = lax.ppermute(core, "tile", [(i, i ^ 1) for i in range(peers)])
    pairs = []
    for i in range(1, peers - 1, 2):
        pairs += [(i, i + 1), (i + 1, i)]
    return got_core, lax.ppermute(other, "tile", pairs)


def layer_exchange(outgoing, up, down):
    peers = lax.axis_size("layer")
    span = outgoing.shape[1] // 3
    partner = lax.ppermute(outgoing, "layer", [(i, i ^ 1) for i in range(peers)])
    above = shifted(jnp.concatenate([partner[:, 2 * span :], up], axis=1), "layer", 2)
    below = shifted(jnp.concatenate([partner[:, :span], down], axis=1), "layer", -2)
    return partner, above, below


def axis_total(x, axis):
    peers = lax.axis_size(axis)
    copies = jnp.broadcast_to(x[None], (peers,) + x.shape)
    return jnp.sum(lax.all_to_all(copies, axis, 0, 0), axis=0)


def local(start, site_weight, onsite, hop_right, hop_down, send_rows, recv_rows, block_counts, inter_blocks):
    count, height, breadth = start.shape
    half, slots, blk = send_rows.shape
    span = 3 * slots * blk
    lower = lax.axis_index("layer") // 2
    tile = lax.axis_index("tile")
    tiles = lax.axis_size("tile")
    info = jnp.stack([tile % 2, (tile != tiles - 1).astype(jnp.int32)])

    def near(table):
        wide = jnp.pad(table, ((1, 1), (0, 0), (0, 0)))
        return lax.dynamic_slice_in_dim(wide, lower, 3, axis=0)

    live = lax.broadcasted_iota(jnp.int32, send_rows.shape, 1) < block_counts[:, :, None]
    sends = near(jnp.where(live, send_rows, -breadth)).reshape(span)
    offset = lower + jnp.arange(3, dtype=jnp.int32)[:, None, None]
    inside = jnp.logical_and(offset > 0, offset <= half)
    sends = jnp.where(
        jnp.broadcast_to(inside, (3, slots, blk)).reshape(span), sends, -breadth
    )
    recvs = near(recv_rows).reshape(span)
    index = jnp.stack([sends // breadth, sends % breadth, recvs // breadth, recvs % breadth])
    index = jnp.concatenate([index, jnp.zeros((4, span), jnp.int32)], axis=0)
    blocks = jnp.concatenate(
        [
            lax.dynamic_index_in_dim(inter_blocks, jnp.clip(lower + d, 0, half - 1), 0, False)
            for d in (-1, 0, 1)
        ],
        axis=0,
    )
    turned = start.transpose(1, 0, 2)

    def of(shape, dtype=F32):
        return jax.ShapeDtypeStruct(shape, dtype)

    rim0 = of((16, height * count), BF16)
    core, other = call(pre_body, (rim0, rim0))(info, turned, site_weight, hop_right)
    core, other = tile_swaps(core, other)
    state = of((height, 2 * count, breadth))
    flow_shape = of((height, count, breadth))
    outgoing_shape = of((2 * count, span), BF16)
    face = of((2 * count, breadth), BF16)
    cells_scratch = pltpu.VMEM((height, 2 * count, breadth), BF16)
    lhs_scratch = pltpu.VMEM((height, 2 * count, span), BF16)
    panel, hop_left, term, flow, outgoing, up, down = call(
        init_body,
        (
            state,
            of((height, breadth)),
            state,
            flow_shape,
            outgoing_shape,
            of((2 * count, 2 * breadth), BF16),
            face,
        ),
        (cells_scratch,),
    )(info, turned, site_weight, onsite, hop_right, hop_down, core, other, index)
    panels, flows = [panel], [flow]
    bond_rows = None
    rim = of((16, height * 2 * count), BF16)
    for step in range(ORDER):
        partner, above, below = layer_exchange(outgoing, up, down)
        if step > 0:
            core, other = tile_swaps(core, other)
            term, flow = call(near_body, (state, flow_shape))(
                info, panels[-1], onsite, hop_right, hop_left, hop_down, core, other
            )
            flows.append(flow)
        if bond_rows is None:
            bond_rows = above
        previous = panels[-2] if step else panels[-1]
        args = (info, term, previous, partner, above, below, bond_rows, hop_down, blocks, index)
        if step < ORDER - 1:
            panel, outgoing, core, other, up, down = call(
                functools.partial(far_body, step),
                (state, outgoing_shape, rim, rim, face, face),
                (lhs_scratch, cells_scratch),
            )(*args)
            panels.append(panel)
        else:
            moments = call(moment_body, of((ORDER * ORDER, 128)), scalars=0)(*panels, *flows)
            moments = axis_total(axis_total(moments, "tile"), "layer")
            final = call(
                functools.partial(far_body, step),
                of((height, 2 * count, breadth), BF16),
                (lhs_scratch,),
            )(*args)
    cells = count * height * breadth * lax.axis_size("layer") * tiles
    moments = jnp.sum(moments, axis=1).reshape(ORDER, ORDER) * (-0.25 / cells)
    return final.transpose(1, 0, 2), moments


def solution(mesh):
    return jax.shard_map(
        local,
        mesh=mesh,
        in_specs=(
            P(None, "layer", "tile"),
            P("layer", "tile"),
            P("layer", "tile"),
            P("layer", "tile"),
            P("layer", "tile"),
            P("layer", "tile", None),
            P("layer", "tile", None),
            P("layer", "tile"),
            P("layer", "tile", None, None),
        ),
        out_specs=(P(None, "layer", "tile"), P()),
        check_vma=False,
    )
```

time: 507 us -> 144 us (0.28)
  the two profiles are of different devices: /device:TPU:96 before, /device:TPU:32 now
where the time goes in v1:
time: 144 us; the launch traced here: 143 us
  starting transfers between devices  97.5 us (68%)
  waiting for transfers between devices  22 us (15%)
  Pallas kernels  15.1 us (10%)
  local copies, waits for them, and re-layouts  6.97 us (5%)
    all_to_all x2, starting transfers between devices, axis_total(): return jnp.sum(lax.all_to_all(copies, axis, 0, 0), axis=0)  31.5 us
    ppermute x8, starting transfers between devices, shifted(): return lax.ppermute(x, axis, pairs)  28.6 us
    ppermute x4, starting transfers between devices, layer_exchange(): lax.ppermute(outgoing, 'layer', [(i, i ^ 1) for i in range(peers)])  17.4 us
    ppermute x4, starting transfers between devices, tile_swaps(): got_core = lax.ppermute(core, 'tile', [(i, i ^ 1) for i in range(peers)])  17.3 us
    pallas_call x10, Pallas kernels, run(): pl.pallas_call(body, out_shape=outs, in_specs=specs, out_specs=jax.tree.m...  15.1 us
    all_to_all x2, waiting for transfers between devices, axis_total(): return jnp.sum(lax.all_to_all(copies, axis, 0, 0), axis=0)  8.59 us
    ppermute x4, waiting for transfers between devices, layer_exchange(): lax.ppermute(outgoing, 'layer', [(i, i ^ 1) for i in range(peers)])  7.43 us
    ppermute x8, waiting for transfers between devices, shifted(): return lax.ppermute(x, axis, pairs)  5.23 us
  transfers between devices with their start and end apart: 22, of which 11 were waited for; matrix products, arithmetic and copies ran while one was open for 2% of the time, Pallas kernels for 2%

profile of v1, /device:TPU:32, one launch (start us, length us, event | category | flops | bytes accessed | tf_op | source)
XLA Modules:
  0.0 143.3 jit_solution(16766837291804136991)
XLA Ops:
  2.6 2.0 %collective-permute-start = (bf16[16,256]{1,0:T(8,128)(2,1)S(1)}, bf16[16,256]{1,0:T(8,128)(2,1)S(1)}, u32[]{:S(2)}, u32[]{:S(2)}) collective-permute-start(bf16[16,256]{1,0:T(8,128)(2,1)S(1)} %get-tuple-element.35), channel_id=1, source_target_pairs={{0,1},{1,0},{2,3},{3,2},{4,5},{5,4},{6,7},{7,6},{8,9},{9,8},{10,11... | collective-permute-start | bytes 24584 | tf_op jit(solution)/shard_map/ppermute | solution.py:323
  7.6 1.8 %shard_map.105 = (f32[16,32,256]{2,1,0:T(8,128)S(1)}, f32[16,256]{1,0:T(8,128)S(1)}, f32[16,32,256]{2,1,0:T(8,128)S(1)}, f32[16,16,256]{2,1,0:T(8,128)S(1)}, bf1...) custom-call(s32[2]{0:T(128)S(1)} %pad_add_fusion.info_ref, ...), custom_call_target="tpu_custom_call" | custom-call | tf_op jit(solution)/shard_map/pallas_call | solution.py:27
  9.5 7.4 %collective-permute-start.2 = (bf16[32,1536]{1,0:T(8,128)(2,1)S(1)}, bf16[32,1536]{1,0:T(8,128)(2,1)S(1)}, u32[]{:S(2)}, u32[]{:S(2)}) collective-permute-start(bf16[32,1536]{1,0:T(8,128)(2,1)S(1)} %get-tuple-element.39), channel_id=1, source_target_pairs={{0,32},{32,0},{64,96},{96,64},{128,160},{160,128},{192,224},{224,1... | collective-permute-start | bytes 294920 | tf_op jit(solution)/shard_map/ppermute | solution.py:333
  16.9 1.1 dynamic-slice_bitcast_fusion.2
  17.9 1.5 %collective-permute-done.2.partner_ref = bf16[32,1536]{1,0:T(8,128)(2,1)S(1)} collective-permute-done((bf16[32,1536]{1,0:T(8,128)(2,1)S(1)}, bf16[32,1536]{1,0:T(8,128)(2,1)S(1)}, u32[]{:S(2)}, u32[]{:S(2)}) %collective-permute-start.2) | collective-permute-done | bytes 98336 | tf_op jit(solution)/shard_map/ppermute | solution.py:333
  19.5 1.3 collective-permute-start.4
  20.8 5.4 %collective-permute-start.3 = (bf16[32,1024]{1,0:T(8,128)(2,1)S(1)}, bf16[32,1024]{1,0:T(8,128)(2,1)S(1)}, u32[]{:S(2)}, u32[]{:S(2)}) collective-permute-start(bf16[32,1024]{1,0:T(8,128)(2,1)S(1)} %pad_maximum_fusion.1), channel_id=1, source_target_pairs={{0,64},{32,96},{64,128},{96,160},{128,192},{160,224},{192,256},{22... | collective-permute-start | bytes 196616 | tf_op jit(solution)/shard_map/ppermute | solution.py:318
  26.3 2.1 %collective-permute-done.3.above_ref.bond_ref = bf16[32,1024]{1,0:T(8,128)(2,1)S(1)} collective-permute-done((bf16[32,1024]{1,0:T(8,128)(2,1)S(1)}, bf16[32,1024]{1,0:T(8,128)(2,1)S(1)}, u32[]{:S(2)}, u32[]{:S(2)}) %collective-permute-start.3) | collective-permute-done | bytes 65568 | tf_op jit(solution)/shard_map/ppermute | solution.py:318
  28.5 2.5 %shard_map.106 = (f32[16,32,256]{2,1,0:T(8,128)S(1)}, bf16[32,1536]{1,0:T(8,128)(2,1)S(1)}, bf16[16,512]{1,0:T(8,128)(2,1)S(1)}, bf16[16,512]{1,0:T(8,128)(2,1)S...) custom-call(s32[2]{0:T(128)S(1)} %pad_add_fusion.info_ref, f32[16,32,256]{2,1,0:T(8,128)S(1)} %get-tuple-element.37.term_ref, ...), custom_call_target="tpu_custom_call" | custom-call | tf_op jit(solution)/shard_map/pallas_call | solution.py:27
  31.0 4.1 %collective-permute-start.7 = (bf16[32,1536]{1,0:T(8,128)(2,1)S(1)}, bf16[32,1536]{1,0:T(8,128)(2,1)S(1)}, u32[]{:S(2)}, u32[]{:S(2)}) collective-permute-start(bf16[32,1536]{1,0:T(8,128)(2,1)S(1)} %get-tuple-element.47), channel_id=1, source_target_pairs={{0,32},{32,0},{64,96},{96,64},{128,160},{160,128},{192,224},{224,1... | collective-permute-start | bytes 294920 | tf_op jit(solution)/shard_map/ppermute | solution.py:333
  35.1 3.1 %collective-permute-done.7.partner_ref = bf16[32,1536]{1,0:T(8,128)(2,1)S(1)} collective-permute-done((bf16[32,1536]{1,0:T(8,128)(2,1)S(1)}, bf16[32,1536]{1,0:T(8,128)(2,1)S(1)}, u32[]{:S(2)}, u32[]{:S(2)}) %collective-permute-start.7) | collective-permute-done | bytes 98336 | tf_op jit(solution)/shard_map/ppermute | solution.py:333
  38.2 1.3 collective-permute-start.9
  39.5 5.9 %collective-permute-start.8 = (bf16[32,768]{1,0:T(8,128)(2,1)S(1)}, bf16[32,768]{1,0:T(8,128)(2,1)S(1)}, u32[]{:S(2)}, u32[]{:S(2)}) collective-permute-start(bf16[32,768]{1,0:T(8,128)(2,1)S(1)} %pad_maximum_fusion.3), channel_id=1, source_target_pairs={{0,64},{32,96},{64,128},{96,160},{128,192},{160,224},{192,256},{22... | collective-permute-start | bytes 147464 | tf_op jit(solution)/shard_map/ppermute | solution.py:318
  45.4 1.9 %collective-permute-start.5 = (bf16[16,512]{1,0:T(8,128)(2,1)S(1)}, bf16[16,512]{1,0:T(8,128)(2,1)S(1)}, u32[]{:S(2)}, u32[]{:S(2)}) collective-permute-start(bf16[16,512]{1,0:T(8,128)(2,1)S(1)} %get-tuple-element.44), channel_id=1, source_target_pairs={{0,1},{1,0},{2,3},{3,2},{4,5},{5,4},{6,7},{7,6},{8,9},{9,8},{10,11... | collective-permute-start | bytes 49160 | tf_op jit(solution)/shard_map/ppermute | solution.py:323
  49.6 2.5 %shard_map.108 = (f32[16,32,256]{2,1,0:T(8,128)S(1)}, bf16[32,1536]{1,0:T(8,128)(2,1)S(1)}, bf16[16,512]{1,0:T(8,128)(2,1)S(1)}, bf16[16,512]{1,0:T(8,128)(2,1)S...) custom-call(s32[2]{0:T(128)S(1)} %pad_add_fusion.info_ref, f32[16,32,256]{2,1,0:T(8,128)S(1)} %get-tuple-element.46.term_ref, ...), custom_call_target="tpu_custom_call" | custom-call | tf_op jit(solution)/shard_map/pallas_call | solution.py:27
  52.1 3.6 %collective-permute-start.12 = (bf16[32,1536]{1,0:T(8,128)(2,1)S(1)}, bf16[32,1536]{1,0:T(8,128)(2,1)S(1)}, u32[]{:S(2)}, u32[]{:S(2)}) collective-permute-start(bf16[32,1536]{1,0:T(8,128)(2,1)S(1)} %get-tuple-element.54), channel_id=1, source_target_pairs={{0,32},{32,0},{64,96},{96,64},{128,160},{160,128},{192,224},{224,1... | collective-permute-start | bytes 294920 | tf_op jit(solution)/shard_map/ppermute | solution.py:333
  55.8 2.9 %collective-permute-done.12.partner_ref = bf16[32,1536]{1,0:T(8,128)(2,1)S(1)} collective-permute-done((bf16[32,1536]{1,0:T(8,128)(2,1)S(1)}, bf16[32,1536]{1,0:T(8,128)(2,1)S(1)}, u32[]{:S(2)}, u32[]{:S(2)}) %collective-permute-start.12) | collective-permute-done | bytes 98336 | tf_op jit(solution)/shard_map/ppermute | solution.py:333
  58.6 1.3 collective-permute-start.14
  60.0 6.7 %collective-permute-start.13 = (bf16[32,768]{1,0:T(8,128)(2,1)S(1)}, bf16[32,768]{1,0:T(8,128)(2,1)S(1)}, u32[]{:S(2)}, u32[]{:S(2)}) collective-permute-start(bf16[32,768]{1,0:T(8,128)(2,1)S(1)} %pad_maximum_fusion.5), channel_id=1, source_target_pairs={{0,64},{32,96},{64,128},{96,160},{128,192},{160,224},{192,256},{22... | collective-permute-start | bytes 147464 | tf_op jit(solution)/shard_map/ppermute | solution.py:318
  66.6 5.3 %collective-permute-start.10 = (bf16[16,512]{1,0:T(8,128)(2,1)S(1)}, bf16[16,512]{1,0:T(8,128)(2,1)S(1)}, u32[]{:S(2)}, u32[]{:S(2)}) collective-permute-start(bf16[16,512]{1,0:T(8,128)(2,1)S(1)} %get-tuple-element.51), channel_id=1, source_target_pairs={{0,1},{1,0},{2,3},{3,2},{4,5},{5,4},{6,7},{7,6},{8,9},{9,8},{10,11... | collective-permute-start | bytes 49160 | tf_op jit(solution)/shard_map/ppermute | solution.py:323
  73.8 2.5 %shard_map.110 = (f32[16,32,256]{2,1,0:T(8,128)S(1)}, bf16[32,1536]{1,0:T(8,128)(2,1)S(1)}, bf16[16,512]{1,0:T(8,128)(2,1)S(1)}, bf16[16,512]{1,0:T(8,128)(2,1)S...) custom-call(s32[2]{0:T(128)S(1)} %pad_add_fusion.info_ref, f32[16,32,256]{2,1,0:T(8,128)S(1)} %get-tuple-element.53.term_ref, ...), custom_call_target="tpu_custom_call" | custom-call | tf_op jit(solution)/shard_map/pallas_call | solution.py:27
  76.3 8.2 %collective-permute-start.15 = (bf16[16,512]{1,0:T(8,128)(2,1)S(1)}, bf16[16,512]{1,0:T(8,128)(2,1)S(1)}, u32[]{:S(2)}, u32[]{:S(2)}) collective-permute-start(bf16[16,512]{1,0:T(8,128)(2,1)S(1)} %get-tuple-element.58), channel_id=1, source_target_pairs={{0,1},{1,0},{2,3},{3,2},{4,5},{5,4},{6,7},{7,6},{8,9},{9,8},{10,11... | collective-permute-start | bytes 49160 | tf_op jit(solution)/shard_map/ppermute | solution.py:323
  85.3 1.0 shard_map.111
  87.5 16.3 %all-to-all-start = ((f32[32,16,128]{2,1,0:T(8,128)}), f32[32,16,128]{2,1,0:T(8,128)S(1)}, u32[]{:S(2)}, u32[]{:S(2)}) async-start(f32[32,16,128]{2,1,0:T(8,128)} %broadcast_in_dim.34), calls=%async_computation | async-start | bytes 524288 | tf_op jit(solution)/shard_map/all_to_all | solution.py:342
  103.8 2.2 %collective-permute-start.17 = (bf16[32,1536]{1,0:T(8,128)(2,1)S(1)}, bf16[32,1536]{1,0:T(8,128)(2,1)S(1)}, u32[]{:S(2)}, u32[]{:S(2)}) collective-permute-start(bf16[32,1536]{1,0:T(8,128)(2,1)S(1)} %get-tuple-element.61), channel_id=1, source_target_pairs={{0,32},{32,0},{64,96},{96,64},{128,160},{160,128},{192,224},{224,1... | collective-permute-start | bytes 294920 | tf_op jit(solution)/shard_map/ppermute | solution.py:333
  106.0 6.7 %all-to-all-done = f32[32,16,128]{2,1,0:T(8,128)S(1)} async-done(((f32[32,16,128]{2,1,0:T(8,128)}), f32[32,16,128]{2,1,0:T(8,128)S(1)}, u32[]{:S(2)}, u32[]{:S(2)}) %all-to-all-start) | async-done | bytes 262176 | tf_op jit(solution)/shard_map/all_to_all | solution.py:342
  113.4 15.2 %all-to-all-start.1 = ((f32[16,16,128]{2,1,0:T(8,128)}), f32[16,16,128]{2,1,0:T(8,128)S(1)}, u32[]{:S(2)}, u32[]{:S(2)}) async-start(f32[16,16,128]{2,1,0:T(8,128)} %broadcast_in_dim.35), calls=%async_computation.1 | async-start | bytes 262144 | tf_op jit(solution)/shard_map/all_to_all | solution.py:342
  128.6 1.3 collective-permute-start.19
  130.0 5.4 %collective-permute-start.18 = (bf16[32,768]{1,0:T(8,128)(2,1)S(1)}, bf16[32,768]{1,0:T(8,128)(2,1)S(1)}, u32[]{:S(2)}, u32[]{:S(2)}) collective-permute-start(bf16[32,768]{1,0:T(8,128)(2,1)S(1)} %pad_maximum_fusion.7), channel_id=1, source_target_pairs={{0,64},{32,96},{64,128},{96,160},{128,192},{160,224},{192,256},{22... | collective-permute-start | bytes 147464 | tf_op jit(solution)/shard_map/ppermute | solution.py:318
  135.4 3.0 %collective-permute-done.19.below_ref = bf16[32,768]{1,0:T(8,128)(2,1)S(1)} collective-permute-done((bf16[32,768]{1,0:T(8,128)(2,1)S(1)}, bf16[32,768]{1,0:T(8,128)(2,1)S(1)}, u32[]{:S(2)}, u32[]{:S(2)}) %collective-permute-start.19) | collective-permute-done | bytes 49184 | tf_op jit(solution)/shard_map/ppermute | solution.py:318
  138.5 1.3 shard_map.112
  140.6 1.9 %all-to-all-done.1 = f32[16,16,128]{2,1,0:T(8,128)S(1)} async-done(((f32[16,16,128]{2,1,0:T(8,128)}), f32[16,16,128]{2,1,0:T(8,128)S(1)}, u32[]{:S(2)}, u32[]{:S(2)}) %all-to-all-start.1) | async-done | bytes 131104 | tf_op jit(solution)/shard_map/all_to_all | solution.py:342
  (68 shorter events, 13.4 us)
Async XLA Ops:
  0.6 1.1 copy-start.1
  0.7 1.1 copy-start.3
  2.6 4.4 %collective-permute-start = (bf16[16,256]{1,0:T(8,128)(2,1)S(1)}, bf16[16,256]{1,0:T(8,128)(2,1)S(1)}, u32[]{:S(2)}, u32[]{:S(2)}) collective-permute-start(bf16[16,256]{1,0:T(8,128)(2,1)S(1)} %get-tuple-element.35), channel_id=1, source_target_pairs={{0,1},{1,0},{2,3},{3,2},{4,5},{5,4},{6,7},{7,6},{8,9},{9,8},{10,11... | collective-permute-start | bytes 24584 | tf_op jit(solution)/shard_map/ppermute | solution.py:323
  4.6 2.4 %collective-permute-start.1 = (bf16[16,256]{1,0:T(8,128)(2,1)S(1)}, bf16[16,256]{1,0:T(8,128)(2,1)S(1)}, u32[]{:S(2)}, u32[]{:S(2)}) collective-permute-start(bf16[16,256]{1,0:T(8,128)(2,1)S(1)} %get-tuple-element.36), channel_id=1, source_target_pairs={{1,2},{2,1},{3,4},{4,3},{5,6},{6,5},{7,8},{8,7},{9,10},{10,9},{11,... | collective-permute-start | bytes 24584 | tf_op jit(solution)/shard_map/ppermute | solution.py:327
  5.2 0.7 copy-start.4
  5.3 0.7 copy-start.6
  6.0 0.7 copy-start.5
  6.9 0.7 copy-start
  6.9 0.7 copy-start.2
  9.5 10.0 %collective-permute-start.2 = (bf16[32,1536]{1,0:T(8,128)(2,1)S(1)}, bf16[32,1536]{1,0:T(8,128)(2,1)S(1)}, u32[]{:S(2)}, u32[]{:S(2)}) collective-permute-start(bf16[32,1536]{1,0:T(8,128)(2,1)S(1)} %get-tuple-element.39), channel_id=1, source_target_pairs={{0,32},{32,0},{64,96},{96,64},{128,160},{160,128},{192,224},{224,1... | collective-permute-start | bytes 294920 | tf_op jit(solution)/shard_map/ppermute | solution.py:333
  19.5 6.9 %collective-permute-start.4 = (bf16[32,768]{1,0:T(8,128)(2,1)S(1)}, bf16[32,768]{1,0:T(8,128)(2,1)S(1)}, u32[]{:S(2)}, u32[]{:S(2)}) collective-permute-start(bf16[32,768]{1,0:T(8,128)(2,1)S(1)} %pad_maximum_fusion.2), channel_id=1, source_target_pairs={{64,0},{96,32},{128,64},{160,96},{192,128},{224,160},{256,192},{28... | collective-permute-start | bytes 147464 | tf_op jit(solution)/shard_map/ppermute | solution.py:318
  20.8 7.7 %collective-permute-start.3 = (bf16[32,1024]{1,0:T(8,128)(2,1)S(1)}, bf16[32,1024]{1,0:T(8,128)(2,1)S(1)}, u32[]{:S(2)}, u32[]{:S(2)}) collective-permute-start(bf16[32,1024]{1,0:T(8,128)(2,1)S(1)} %pad_maximum_fusion.1), channel_id=1, source_target_pairs={{0,64},{32,96},{64,128},{96,160},{128,192},{160,224},{192,256},{22... | collective-permute-start | bytes 196616 | tf_op jit(solution)/shard_map/ppermute | solution.py:318
  31.0 7.2 %collective-permute-start.7 = (bf16[32,1536]{1,0:T(8,128)(2,1)S(1)}, bf16[32,1536]{1,0:T(8,128)(2,1)S(1)}, u32[]{:S(2)}, u32[]{:S(2)}) collective-permute-start(bf16[32,1536]{1,0:T(8,128)(2,1)S(1)} %get-tuple-element.47), channel_id=1, source_target_pairs={{0,32},{32,0},{64,96},{96,64},{128,160},{160,128},{192,224},{224,1... | collective-permute-start | bytes 294920 | tf_op jit(solution)/shard_map/ppermute | solution.py:333
  38.2 11.4 %collective-permute-start.9 = (bf16[32,768]{1,0:T(8,128)(2,1)S(1)}, bf16[32,768]{1,0:T(8,128)(2,1)S(1)}, u32[]{:S(2)}, u32[]{:S(2)}) collective-permute-start(bf16[32,768]{1,0:T(8,128)(2,1)S(1)} %pad_maximum_fusion.4), channel_id=1, source_target_pairs={{64,0},{96,32},{128,64},{160,96},{192,128},{224,160},{256,192},{28... | collective-permute-start | bytes 147464 | tf_op jit(solution)/shard_map/ppermute | solution.py:318
  39.5 10.1 %collective-permute-start.8 = (bf16[32,768]{1,0:T(8,128)(2,1)S(1)}, bf16[32,768]{1,0:T(8,128)(2,1)S(1)}, u32[]{:S(2)}, u32[]{:S(2)}) collective-permute-start(bf16[32,768]{1,0:T(8,128)(2,1)S(1)} %pad_maximum_fusion.3), channel_id=1, source_target_pairs={{0,64},{32,96},{64,128},{96,160},{128,192},{160,224},{192,256},{22... | collective-permute-start | bytes 147464 | tf_op jit(solution)/shard_map/ppermute | solution.py:318
  45.4 3.1 %collective-permute-start.5 = (bf16[16,512]{1,0:T(8,128)(2,1)S(1)}, bf16[16,512]{1,0:T(8,128)(2,1)S(1)}, u32[]{:S(2)}, u32[]{:S(2)}) collective-permute-start(bf16[16,512]{1,0:T(8,128)(2,1)S(1)} %get-tuple-element.44), channel_id=1, source_target_pairs={{0,1},{1,0},{2,3},{3,2},{4,5},{5,4},{6,7},{7,6},{8,9},{9,8},{10,11... | collective-permute-start | bytes 49160 | tf_op jit(solution)/shard_map/ppermute | solution.py:323
  47.4 1.2 collective-permute-start.6
  52.1 6.5 %collective-permute-start.12 = (bf16[32,1536]{1,0:T(8,128)(2,1)S(1)}, bf16[32,1536]{1,0:T(8,128)(2,1)S(1)}, u32[]{:S(2)}, u32[]{:S(2)}) collective-permute-start(bf16[32,1536]{1,0:T(8,128)(2,1)S(1)} %get-tuple-element.54), channel_id=1, source_target_pairs={{0,32},{32,0},{64,96},{96,64},{128,160},{160,128},{192,224},{224,1... | collective-permute-start | bytes 294920 | tf_op jit(solution)/shard_map/ppermute | solution.py:333
  58.6 15.1 %collective-permute-start.14 = (bf16[32,768]{1,0:T(8,128)(2,1)S(1)}, bf16[32,768]{1,0:T(8,128)(2,1)S(1)}, u32[]{:S(2)}, u32[]{:S(2)}) collective-permute-start(bf16[32,768]{1,0:T(8,128)(2,1)S(1)} %pad_maximum_fusion.6), channel_id=1, source_target_pairs={{64,0},{96,32},{128,64},{160,96},{192,128},{224,160},{256,192},{28... | collective-permute-start | bytes 147464 | tf_op jit(solution)/shard_map/ppermute | solution.py:318
  60.0 13.8 %collective-permute-start.13 = (bf16[32,768]{1,0:T(8,128)(2,1)S(1)}, bf16[32,768]{1,0:T(8,128)(2,1)S(1)}, u32[]{:S(2)}, u32[]{:S(2)}) collective-permute-start(bf16[32,768]{1,0:T(8,128)(2,1)S(1)} %pad_maximum_fusion.5), channel_id=1, source_target_pairs={{0,64},{32,96},{64,128},{96,160},{128,192},{160,224},{192,256},{22... | collective-permute-start | bytes 147464 | tf_op jit(solution)/shard_map/ppermute | solution.py:318
  66.6 6.1 %collective-permute-start.10 = (bf16[16,512]{1,0:T(8,128)(2,1)S(1)}, bf16[16,512]{1,0:T(8,128)(2,1)S(1)}, u32[]{:S(2)}, u32[]{:S(2)}) collective-permute-start(bf16[16,512]{1,0:T(8,128)(2,1)S(1)} %get-tuple-element.51), channel_id=1, source_target_pairs={{0,1},{1,0},{2,3},{3,2},{4,5},{5,4},{6,7},{7,6},{8,9},{9,8},{10,11... | collective-permute-start | bytes 49160 | tf_op jit(solution)/shard_map/ppermute | solution.py:323
  71.9 0.8 collective-permute-start.11
  76.3 9.0 %collective-permute-start.15 = (bf16[16,512]{1,0:T(8,128)(2,1)S(1)}, bf16[16,512]{1,0:T(8,128)(2,1)S(1)}, u32[]{:S(2)}, u32[]{:S(2)}) collective-permute-start(bf16[16,512]{1,0:T(8,128)(2,1)S(1)} %get-tuple-element.58), channel_id=1, source_target_pairs={{0,1},{1,0},{2,3},{3,2},{4,5},{5,4},{6,7},{7,6},{8,9},{9,8},{10,11... | collective-permute-start | bytes 49160 | tf_op jit(solution)/shard_map/ppermute | solution.py:323
  84.5 0.8 collective-permute-start.16
  87.5 25.3 %all-to-all-start = ((f32[32,16,128]{2,1,0:T(8,128)}), f32[32,16,128]{2,1,0:T(8,128)S(1)}, u32[]{:S(2)}, u32[]{:S(2)}) async-start(f32[32,16,128]{2,1,0:T(8,128)} %broadcast_in_dim.34), calls=%async_computation | async-start | bytes 524288 | tf_op jit(solution)/shard_map/all_to_all | solution.py:342
  103.8 24.8 %collective-permute-start.17 = (bf16[32,1536]{1,0:T(8,128)(2,1)S(1)}, bf16[32,1536]{1,0:T(8,128)(2,1)S(1)}, u32[]{:S(2)}, u32[]{:S(2)}) collective-permute-start(bf16[32,1536]{1,0:T(8,128)(2,1)S(1)} %get-tuple-element.61), channel_id=1, source_target_pairs={{0,32},{32,0},{64,96},{96,64},{128,160},{160,128},{192,224},{224,1... | collective-permute-start | bytes 294920 | tf_op jit(solution)/shard_map/ppermute | solution.py:333
  113.4 29.1 %all-to-all-start.1 = ((f32[16,16,128]{2,1,0:T(8,128)}), f32[16,16,128]{2,1,0:T(8,128)S(1)}, u32[]{:S(2)}, u32[]{:S(2)}) async-start(f32[16,16,128]{2,1,0:T(8,128)} %broadcast_in_dim.35), calls=%async_computation.1 | async-start | bytes 262144 | tf_op jit(solution)/shard_map/all_to_all | solution.py:342
  128.6 9.8 %collective-permute-start.19 = (bf16[32,768]{1,0:T(8,128)(2,1)S(1)}, bf16[32,768]{1,0:T(8,128)(2,1)S(1)}, u32[]{:S(2)}, u32[]{:S(2)}) collective-permute-start(bf16[32,768]{1,0:T(8,128)(2,1)S(1)} %pad_maximum_fusion.8), channel_id=1, source_target_pairs={{64,0},{96,32},{128,64},{160,96},{192,128},{224,160},{256,192},{28... | collective-permute-start | bytes 147464 | tf_op jit(solution)/shard_map/ppermute | solution.py:318
  130.0 8.5 %collective-permute-start.18 = (bf16[32,768]{1,0:T(8,128)(2,1)S(1)}, bf16[32,768]{1,0:T(8,128)(2,1)S(1)}, u32[]{:S(2)}, u32[]{:S(2)}) collective-permute-start(bf16[32,768]{1,0:T(8,128)(2,1)S(1)} %pad_maximum_fusion.7), channel_id=1, source_target_pairs={{0,64},{32,96},{64,128},{96,160},{128,192},{160,224},{192,256},{22... | collective-permute-start | bytes 147464 | tf_op jit(solution)/shard_map/ppermute | solution.py:318
